TPU v7x, 128 devices: a whole 4x4x4 slice. The times are simulated.
128 devices in a mesh: rep: 8 (over y, core), shard: 16 (over x, z).
Axes of the slice: x: 4, y: 4, z: 4, core: 2. Of those that a mesh axis runs over, the one named last changes fastest.
Arguments:
- tokens: bfloat16 [16384, 1024], P(('rep', 'shard')), may hold values from -6 to 6
- doc_ids: int32 [16384], P(('rep', 'shard')), may hold values from -1 to 2, as said below
- grad_out: bfloat16 [16384, 1024], P(('rep', 'shard')), may hold values from -6 to 6
- norm_gains: bfloat16 [2, 2, 1024], P(None, None, 'shard'), may hold values from 0.25 to 1.75
- shifts: bfloat16 [2, 4, 1024], P(None, None, 'shard'), may hold values from -2 to 2
- qkv_weight: bfloat16 [2, 1024, 3072], P(None, 'shard'), may hold values from -0.1875 to 0.1875
- qkv_bias: bfloat16 [2, 3072], P(None, 'shard'), may hold values from -2 to 2
- dense_weight: bfloat16 [2, 1024, 1024], P(None, 'shard'), may hold values from -0.5 to 0.5
- up_weight: bfloat16 [2, 1024, 4096], P(None, 'shard'), may hold values from -0.1875 to 0.1875
- up_bias: bfloat16 [2, 4096], P(None, 'shard'), may hold values from -2 to 2
- down_weight: bfloat16 [2, 4096, 1024], P(None, 'shard'), may hold values from -0.09375 to 0.09375
Outputs:
- output: bfloat16 [16384, 1024], P(('rep', 'shard'))
- input_grad: float32 [16384, 1024], P(('rep', 'shard'))
- grad_norm_gains: float32 [2, 2, 1024], P(None, None, 'shard')
- grad_shifts: float32 [2, 4, 1024], P(None, None, 'shard')
- grad_qkv_weight: float32 [2, 1024, 3072], P(None, 'shard')
- grad_qkv_bias: float32 [2, 3072], P(None, 'shard')
- grad_dense_weight: float32 [2, 1024, 1024], P(None, 'shard')
- grad_up_weight: float32 [2, 1024, 4096], P(None, 'shard')
- grad_up_bias: float32 [2, 4096], P(None, 'shard')
- grad_down_weight: float32 [2, 4096, 1024], P(None, 'shard')
Inputs may be any that keep to these rules, and one draw needn't show every extreme that they name: `doc_ids`: within each aligned block of 128 slots (one device's), the ids start at 0 in the first slot, never fall, and are followed by -1 in the unused slots; at least half of a block's slots are used, and in some block all are.
All inputs are finite; a program needn't handle non-finite values.
Results may differ from a plain program's by a relative error of at most 0.02.
Values may be sent and summed in bfloat16 or wider, within the bound.
No kernel may reach another device: no remote copies, remote signals or barrier semaphores. Data moves between devices by JAX's collectives and lax.ppermute only.
A program may use at most 192 MiB of HBM per device.

v0:
```python
import math

import jax
import jax.numpy as jnp
import numpy as np
from jax import lax
from jax.experimental import pallas as pl
from jax.experimental.pallas import tpu as pltpu
from jax.sharding import PartitionSpec as P

HEADS = 16
HEAD_DIM = 64
ROT = 16
LAYERS = 2
D = 1024
FF = 4096
TOK = 128
REPS = 8
SHARDS = 16
ROWS = REPS * TOK
QKV_R = 3 * D // REPS
FF_R = FF // REPS
A_LANES = QKV_R + FF_R
UNIT = FF // SHARDS // REPS
STEP = 256
EPS = 1e-05
LARGE = 58 * 2**20
SMALL = 24 * 2**20

BF = jnp.bfloat16
F32 = jnp.float32


def take_y(k):
    return [(((y + k) % 4) * 2 + c, y * 2 + c) for y in range(4) for c in range(2)]


CORE_FLIP = [(y * 2 + 1 - c, y * 2 + c) for y in range(4) for c in range(2)]


def fetch_y(a, k):
    return lax.ppermute(a, "rep", take_y(k % 4))


def flip_core(a):
    return lax.ppermute(a, "rep", CORE_FLIP)


Y_GROUPS = [[0, 2, 4, 6], [1, 3, 5, 7]]


def along_y(a):
    return lax.all_to_all(a, "rep", 0, 0, axis_index_groups=Y_GROUPS, tiled=True)


def gather_rep(block):
    near = [block] + [fetch_y(block, k) for k in (1, 2, 3)]
    return near + [flip_core(piece) for piece in near]


def in_y_order(pieces, y):
    near = jnp.zeros((4,) + pieces[0].shape, pieces[0].dtype)
    for k in range(4):
        near = lax.dynamic_update_slice_in_dim(near, pieces[k][None], (y + k) % 4, 0)
    return near


def scatter_rep(near, far):
    own, *sent = join(near, flip_core(far))
    return own, [fetch_y(sent[k - 1], -k) for k in (1, 2, 3)]


def total_of(own, moved):
    for piece in moved:
        own = own + piece.astype(F32)
    return own


def exchange_shard(a):
    return lax.all_to_all(a, "shard", 0, 0, tiled=True)


def add_up(pieces):
    return jnp.sum(pieces.astype(F32), axis=0).astype(BF)


DENSE_IN = [((s % 8) * 16 + 2 * r + s // 8, r * 16 + s) for r in range(REPS) for s in range(SHARDS)]
DENSE_OUT = [((s // 2) * 16 + 8 * (s % 2) + r, r * 16 + s) for r in range(REPS) for s in range(SHARDS)]


def dot(a, b):
    return lax.dot_general(a, b, (((1,), (0,)), ((), ())), preferred_element_type=F32)


def dot_nt(a, b):
    return lax.dot_general(a, b, (((1,), (1,)), ((), ())), preferred_element_type=F32)


def dot_tn(a, b):
    return lax.dot_general(a, b, (((0,), (0,)), ((), ())), preferred_element_type=F32)


def params(limit=SMALL):
    return pltpu.CompilerParams(vmem_limit_bytes=limit)


VMEM = pl.BlockSpec(memory_space=pltpu.VMEM)
SMEM = pl.BlockSpec(memory_space=pltpu.SMEM)


def pack_kernel(place_ref, *refs):
    qkv_refs, up_refs, (down_ref, gains_ref, moves_ref, qkv_bias_ref, up_bias_ref, first_ref, a1_ref, b_ref, a_ref) = refs[:3], refs[3:19], refs[19:]
    r, s = place_ref[0], place_ref[1]
    lane = lax.broadcasted_iota(jnp.int32, (64, 128), 1)
    row = lax.broadcasted_iota(jnp.int32, (64, 128), 0)
    for layer in range(LAYERS):
        for part in range(3):
            a_ref[layer, :, part * 128 : (part + 1) * 128] = qkv_refs[part][layer]
        for group in range(4):
            merged = jnp.zeros((64, 128), F32)
            for sub in range(4):
                piece = up_refs[4 * group + sub][layer].astype(F32)
                turned = pltpu.roll(piece, (32 * sub + 128 - 32 * (r % 4)) % 128, 1)
                merged = jnp.where(lane // 32 == sub, turned, merged)
            low = QKV_R + group * 128
            a_ref[layer, :, low : low + 128] = merged.astype(BF)
        b_ref[layer] = down_ref[layer]
        gains, moves = gains_ref[layer].astype(F32), moves_ref[layer].astype(F32)
        bias = qkv_bias_ref[layer : layer + 1].astype(F32)
        side = jnp.zeros((64, 128), F32)
        for vector, values in enumerate((gains[0:1], moves[0:1], gains[1:2], moves[1:2], moves[2:3], moves[3:4])):
            here = (row == 8 * vector + s // 2) & (lane // 64 == s % 2)
            side = jnp.where(here, jnp.concatenate([values, values], axis=1), side)
        for third in range(3):
            block = 3 * s + third
            target = jnp.where((block // 2) % 8 == r, 48 + block // 16, -1)
            here = (row == target) & (lane // 64 == block % 2)
            values = bias[:, 64 * third : 64 * (third + 1)]
            side = jnp.where(here, jnp.concatenate([values, values], axis=1), side)
        bias = up_bias_ref[layer : layer + 1].astype(F32)
        piece = jnp.where(r // 4 == 0, bias[:, :128], bias[:, 128:])
        turned = pltpu.roll(jnp.broadcast_to(piece, (64, 128)), (32 * (s % 4) + 128 - 32 * (r % 4)) % 128, 1)
        side = jnp.where((row == 51 + s // 4) & (lane // 32 == s % 4), turned, side)
        a_ref[layer, :, A_LANES:] = side.astype(BF)
    first_ref[...] = jnp.broadcast_to(a_ref[0][None], (SHARDS, 64, D))
    a1_ref[...] = a_ref[1]


def pack(place, qkv_weight, up_weight, down_weight, *vectors):
    def lanes(at):
        return pl.BlockSpec((LAYERS, 64, 128), lambda i, place: (0, 0, at(place[0])))

    def whole(a):
        return pl.BlockSpec(a.shape, lambda i, place: (0,) * a.ndim)

    return pl.pallas_call(
        pack_kernel,
        grid_spec=pltpu.PrefetchScalarGridSpec(
            num_scalar_prefetch=1,
            grid=(1,),
            in_specs=[lanes(lambda r, p=p: 8 * p + r) for p in range(3)]
            + [lanes(lambda r, o=o: 2 * o + r // 4) for o in range(16)]
            + [pl.BlockSpec((LAYERS, UNIT, D), lambda i, place: (0, place[0], 0))]
            + [whole(a) for a in vectors],
            out_specs=[
                pl.BlockSpec((SHARDS, 64, D), lambda i, place: (0, 0, 0)),
                pl.BlockSpec((64, D), lambda i, place: (0, 0)),
                pl.BlockSpec((LAYERS, UNIT, D), lambda i, place: (0, 0, 0)),
            ],
            scratch_shapes=[pltpu.VMEM((LAYERS, 64, D), BF)],
        ),
        out_shape=[
            jax.ShapeDtypeStruct((SHARDS, 64, D), BF),
            jax.ShapeDtypeStruct((64, D), BF),
            jax.ShapeDtypeStruct((LAYERS, UNIT, D), BF),
        ],
        compiler_params=params(LARGE),
        name="pack",
    )(place, *[qkv_weight] * 3, *[up_weight] * 16, down_weight, *vectors)


def put_inside(piece, r, qkv_ref, layer):
    for part in range(3):
        low = part * D + 128 * r
        qkv_ref[layer, :, low : low + 128] = piece[:, part * 128 : (part + 1) * 128]


def put_up(whole, up_ref, layer):
    lane = lax.broadcasted_iota(jnp.int32, (64, 128), 1)
    for s in range(SHARDS):
        group, sub = s // 4, s % 4
        for half in range(2):
            merged = jnp.zeros((64, 128), F32)
            for inner_r in range(4):
                piece = whole[4 * half + inner_r][:, group * 128 : (group + 1) * 128]
                shift = (32 * inner_r - 32 * sub) % 128
                turned = pltpu.roll(piece, shift, 1) if shift else piece
                merged = jnp.where(lane // 32 == inner_r, turned, merged)
            low = 256 * s + 128 * half
            up_ref[layer, :, low : low + 128] = merged


def put_layer(place_ref, near_ref, far_ref, qkv_ref, up_ref, down_ref, dense_ref=None):
    c = place_ref[0] % 2
    whole = []
    for r in range(REPS):
        piece = jnp.where(c == r % 2, near_ref[r // 2], far_ref[r // 2]).astype(F32)
        put_inside(piece[:64], r, qkv_ref, 0)
        whole.append(piece[:64, QKV_R:A_LANES])
        down_ref[0, UNIT * r : UNIT * (r + 1), :] = piece[64:96]
        if dense_ref is not None:
            dense_ref[1, 8 * r : 8 * r + 8, :] = piece[96:104]
            dense_ref[0, 8 * r : 8 * r + 8, :] = piece[112:120]
    put_up(whole, up_ref, 0)


def unpack_late_kernel(place_ref, near_ref, far_ref, qkv_in, up_in, down_in, *out_refs):
    put_layer(place_ref, near_ref, far_ref, *out_refs)


UNPACKED = [
    jax.ShapeDtypeStruct((LAYERS, 64, 3 * D), F32),
    jax.ShapeDtypeStruct((LAYERS, 64, FF), F32),
    jax.ShapeDtypeStruct((LAYERS, 256, D), F32),
]


def layer_specs(layer):
    return [pl.BlockSpec((1,) + a.shape[1:], lambda i: (layer, 0, 0)) for a in UNPACKED]


def unpack_early(place, near, far):
    return pl.pallas_call(
        put_layer,
        grid=(1,),
        in_specs=[SMEM, VMEM, VMEM],
        out_specs=layer_specs(1),
        out_shape=UNPACKED,
        compiler_params=params(),
        name="unpack_early",
    )(place, near, far)


def unpack_late(place, near, far, *filled):
    return pl.pallas_call(
        unpack_late_kernel,
        grid=(1,),
        in_specs=[SMEM, VMEM, VMEM] + [pl.BlockSpec(memory_space=pl.ANY)] * 3,
        out_specs=layer_specs(0) + [VMEM],
        out_shape=UNPACKED + [jax.ShapeDtypeStruct((LAYERS, 64, D), F32)],
        input_output_aliases={3: 0, 4: 1, 5: 2},
        compiler_params=params(),
        name="unpack_late",
    )(place, near, far, *filled)


def join_kernel(near_ref, far_ref, own_ref, *sent_refs):
    for k in range(4):
        rows = slice(k * TOK, (k + 1) * TOK)
        both = near_ref[rows].astype(F32) + far_ref[rows].astype(F32)
        if k == 0:
            own_ref[...] = both
        else:
            sent_refs[k - 1][...] = both.astype(BF)


def join(near, far):
    sent = jax.ShapeDtypeStruct((TOK, D), BF)
    return pl.pallas_call(
        join_kernel,
        in_specs=[VMEM, VMEM],
        out_specs=[VMEM] * 4,
        out_shape=[jax.ShapeDtypeStruct((TOK, D), F32), sent, sent, sent],
        compiler_params=params(),
        name="join",
    )(near, far)


def rotary_table():
    angle = np.arange(TOK, dtype=np.float64)[:, None] * (10000.0 ** (-2.0 * np.arange(8) / ROT))[None, :]
    lane = np.arange(128) % HEAD_DIM
    cos_n = np.where(lane[None, :] < ROT, np.cos(angle)[:, lane % 8], 1.0)
    low_n = np.where(lane[None, :] < 8, -np.sin(angle)[:, lane % 8], 0.0)
    high_n = np.where((lane[None, :] >= 8) & (lane[None, :] < ROT), np.sin(angle)[:, lane % 8], 0.0)
    rest = np.concatenate([cos_n, low_n, high_n], axis=1).astype(np.float32)
    parts = []
    for _ in range(3):
        parts.append(rest.astype(BF))
        rest = rest - parts[-1].astype(np.float32)
    return np.stack(parts)


def tables_kernel(table_ref, *refs):
    pieces, (mask_ref, cos_ref, low_ref, high_ref) = refs[:REPS], refs[REPS:]
    row = lax.broadcasted_iota(jnp.int32, (TOK, TOK), 0)
    col = lax.broadcasted_iota(jnp.int32, (TOK, TOK), 1)
    for block in range(REPS):
        rows = slice(block * TOK, (block + 1) * TOK)
        docs = jnp.broadcast_to(pieces[block][...].astype(F32)[0:1], (TOK, TOK))
        mask = jnp.where((docs == docs.T) & (col <= row), 1.0, 0.0)
        mask_ref[rows] = mask
        places = jnp.sum(mask, axis=1, keepdims=True) - 1.0
        chosen = jnp.where(col.astype(F32) == places, 1.0, 0.0).astype(BF)
        found = dot(chosen, table_ref[0]) + dot(chosen, table_ref[1]) + dot(chosen, table_ref[2])
        cos_ref[rows] = found[:, :128]
        low_ref[rows] = found[:, 128:256]
        high_ref[rows] = found[:, 256:]


def token_tables(opened):
    return pl.pallas_call(
        tables_kernel,
        grid=(1,),
        in_specs=[VMEM] + [pl.BlockSpec((16, 128), lambda i: (16, 0))] * REPS,
        out_specs=[VMEM] * 4,
        out_shape=[jax.ShapeDtypeStruct((ROWS, 128), F32)] * 4,
        compiler_params=params(),
        name="tables",
    )(jnp.asarray(rotary_table()), *opened)


def turn(values, cos_t, low_t, high_t):
    return values * cos_t + pltpu.roll(values, 120, 1) * low_t + pltpu.roll(values, 8, 1) * high_t


def turn_back(values, cos_t, low_t, high_t):
    return values * cos_t - pltpu.roll(values, 120, 1) * low_t - pltpu.roll(values, 8, 1) * high_t


def row_spec(lanes):
    return pl.BlockSpec((STEP, lanes), lambda i: (i, 0))


def whole_spec(shape):
    return pl.BlockSpec(shape, lambda i: (0,) * len(shape))


PROB_SPEC = pl.BlockSpec((STEP // TOK, 2, TOK, TOK), lambda i: (i, 0, 0, 0))
WA_SPEC = whole_spec((SHARDS, 64, D))
HELD = [pltpu.VMEM((FF_R, D), BF), pltpu.VMEM((128, D), BF)]


def wb_specs(at):
    return [pl.BlockSpec((SHARDS, 16, D), lambda i, k=k: (0, at + k, 0)) for k in range(3)]


def hold_weights(wb_refs, wd_ref, wo_ref):
    @pl.when(pl.program_id(0) == 0)
    def _():
        rows = jnp.concatenate([wb_refs[0][...], wb_refs[1][...]], axis=1)
        wd_ref[...] = rows.reshape(FF_R, D)
        wo_ref[...] = wb_refs[2][...].astype(F32)[:, :8].reshape(128, D).astype(BF)


VEC_SPEC = whole_spec((16, D))
NEAR_SPEC = pl.BlockSpec((STEP, D), lambda i: (jnp.minimum(i, 1), 0))
FAR_SPEC = pl.BlockSpec((STEP, D), lambda i: (jnp.maximum(i - 2, 0), 0))


def rows_of(lanes, dtype):
    return jax.ShapeDtypeStruct((ROWS, lanes), dtype)


def put_block(near_ref, far_ref, values):
    @pl.when(pl.program_id(0) < 2)
    def _():
        near_ref[...] = values

    @pl.when(pl.program_id(0) >= 2)
    def _():
        far_ref[...] = values


def inner_kernel(*refs):
    pieces, (wa_ref, mask_ref, cos_ref, low_ref, high_ref) = refs[:REPS], refs[REPS : REPS + 5]
    xh_ref, qkv_ref, prob_ref, o_ref, act_ref, slope_ref, vec_ref = refs[REPS + 5 :]

    @pl.when(pl.program_id(0) == 0)
    def _():
        side = jnp.zeros((64, 128), F32)
        for shard in range(SHARDS):
            side = side + wa_ref[shard, :, A_LANES:].astype(F32)
        vec_ref[...] = jnp.zeros_like(vec_ref)
        for vector in range(6):
            for j in range(8):
                vec_ref[vector : vector + 1, 128 * j : 128 * (j + 1)] = side[8 * vector + j : 8 * vector + j + 1]
        for j in range(7):
            vec_ref[6:7, 128 * j : 128 * (j + 1)] = side[48 + j : 49 + j]

    for step in range(4):

        @pl.when(pl.program_id(0) == step)
        def _(step=step):
            xh_ref[:TOK] = pieces[2 * step][...]
            xh_ref[TOK:] = pieces[2 * step + 1][...]

    xh = xh_ref[...].astype(F32)
    h1 = (xh * vec_ref[0:1] + vec_ref[1:2]).astype(BF)
    h2 = (xh * vec_ref[2:3] + vec_ref[3:4]).astype(BF)
    mixed = dot(h1, wa_ref[:, :, :QKV_R].reshape(D, QKV_R)) + vec_ref[6:7, :QKV_R]
    tables = (cos_ref[...], low_ref[...], high_ref[...])
    q = turn(mixed[:, :128], *tables).astype(BF)
    k = turn(mixed[:, 128:256], *tables).astype(BF)
    v = mixed[:, 256:].astype(BF)
    qkv_ref[:, :128] = q
    qkv_ref[:, 128:256] = k
    qkv_ref[:, 256:] = v
    u = dot(h2, wa_ref[:, :, QKV_R:A_LANES].reshape(D, FF_R)) + vec_ref[6:7, QKV_R:A_LANES]
    share = 0.5 * (1.0 + lax.erf(u * math.sqrt(0.5)))
    act_ref[...] = (u * share).astype(BF)
    slope_ref[...] = share + u * jnp.exp(-0.5 * u * u) * (1.0 / math.sqrt(2.0 * math.pi))
    first = lax.broadcasted_iota(jnp.int32, (TOK, 128), 1) < HEAD_DIM
    zero = jnp.zeros((TOK, 128), BF)
    for block in range(STEP // TOK):
        rows = slice(block * TOK, (block + 1) * TOK)
        allowed = mask_ref[rows] > 0.5
        out = jnp.zeros((TOK, 128), F32)
        for head in range(2):
            mine = first if head == 0 else jnp.logical_not(first)
            scores = dot_nt(jnp.where(mine, q[rows], zero), k[rows]) * HEAD_DIM**-0.5
            scores = jnp.where(allowed, scores, -1e30)
            raised = jnp.exp(scores - jnp.max(scores, axis=-1, keepdims=True))
            prob = raised / jnp.sum(raised, axis=-1, keepdims=True)
            prob_ref[block, head] = prob
            out = out + dot(prob.astype(BF), jnp.where(mine, v[rows], zero))
        o_ref[rows] = out.astype(BF)


def inner(blocks, wa, masks):
    return pl.pallas_call(
        inner_kernel,
        grid=(ROWS // STEP,),
        in_specs=[whole_spec((TOK, D))] * REPS + [WA_SPEC] + [row_spec(128)] * 4,
        out_specs=[row_spec(D), row_spec(QKV_R), PROB_SPEC, row_spec(128), row_spec(FF_R), row_spec(FF_R), VEC_SPEC],
        out_shape=[
            rows_of(D, BF),
            rows_of(QKV_R, BF),
            jax.ShapeDtypeStruct((REPS, 2, TOK, TOK), F32),
            rows_of(128, BF),
            rows_of(FF_R, BF),
            rows_of(FF_R, F32),
            jax.ShapeDtypeStruct((16, D), F32),
        ],
        compiler_params=params(LARGE),
        name="inner",
    )(*blocks, wa, *masks)


HALF = jax.ShapeDtypeStruct((ROWS // 2, D), BF)


def outer_kernel(o_ref, act_ref, down0_ref, down1_ref, dense_ref, near_ref, far_ref, wd_ref, wo_ref):
    hold_weights((down0_ref, down1_ref, dense_ref), wd_ref, wo_ref)
    part = dot(o_ref[...], wo_ref[...]) + dot(act_ref[...], wd_ref[...])
    put_block(near_ref, far_ref, part.astype(BF))


def outer(attended, act, wb, at):
    return pl.pallas_call(
        outer_kernel,
        grid=(ROWS // STEP,),
        in_specs=[row_spec(128), row_spec(FF_R)] + wb_specs(at),
        out_specs=[NEAR_SPEC, FAR_SPEC],
        out_shape=[HALF, HALF],
        scratch_shapes=HELD,
        compiler_params=params(),
        name="outer",
    )(attended, act, wb, wb, wb)


def backward_kernel(
    e_ref, xh_ref, qkv_ref, prob_ref, slope_ref, wa_ref, down0_ref, down1_ref, dense_ref, vec_ref, cos_ref, low_ref, high_ref,
    near_ref, far_ref, dc_ref, du_ref, side_ref, wd_ref, wo_ref,
):
    def add_row(at, values):
        for j in range(values.shape[1] // 128):
            side_ref[at + j : at + j + 1] += values[:, 128 * j : 128 * (j + 1)]

    @pl.when(pl.program_id(0) == 0)
    def _():
        side_ref[...] = jnp.zeros_like(side_ref)

    hold_weights((down0_ref, down1_ref, dense_ref), wd_ref, wo_ref)
    e = e_ref[...]
    add_row(32, jnp.sum(e.astype(F32), axis=0, keepdims=True))
    du = (dot_nt(e, wd_ref[...]) * slope_ref[...]).astype(BF)
    du_ref[...] = du
    grad_o = dot_nt(e, wo_ref[...]).astype(BF)
    tables = (cos_ref[...], low_ref[...], high_ref[...])
    first = lax.broadcasted_iota(jnp.int32, (TOK, 128), 1) < HEAD_DIM
    zero = jnp.zeros((TOK, 128), BF)
    grads = ([], [], [])
    for block in range(STEP // TOK):
        rows = slice(block * TOK, (block + 1) * TOK)
        q, k, v = qkv_ref[rows, :128], qkv_ref[rows, 128:256], qkv_ref[rows, 256:]
        dq = jnp.zeros((TOK, 128), F32)
        dk = jnp.zeros((TOK, 128), F32)
        dv = jnp.zeros((TOK, 128), F32)
        for head in range(2):
            mine = first if head == 0 else jnp.logical_not(first)
            prob = prob_ref[block, head]
            grad_head = jnp.where(mine, grad_o[rows], zero)
            dv = dv + dot_tn(prob.astype(BF), grad_head)
            grad_prob = dot_nt(grad_head, v)
            inner_sum = jnp.sum(prob * grad_prob, axis=-1, keepdims=True)
            ds = (prob * (grad_prob - inner_sum)).astype(BF)
            dq = dq + dot(ds, jnp.where(mine, k, zero))
            dk = dk + dot_tn(ds, jnp.where(mine, q, zero))
        grads[0].append(dq * HEAD_DIM**-0.5)
        grads[1].append(dk * HEAD_DIM**-0.5)
        grads[2].append(dv)
    dq, dk, dv = (jnp.concatenate(g, axis=0) for g in grads)
    dc = jnp.concatenate([turn_back(dq, *tables), turn_back(dk, *tables), dv], axis=1).astype(BF)
    dc_ref[...] = dc
    dh1 = dot_nt(dc, wa_ref[:, :, :QKV_R].reshape(D, QKV_R))
    dh2 = dot_nt(du, wa_ref[:, :, QKV_R:A_LANES].reshape(D, FF_R))
    put_block(near_ref, far_ref, (dh1 * vec_ref[0:1] + dh2 * vec_ref[2:3]).astype(BF))
    xh = xh_ref[...].astype(F32)
    add_row(0, jnp.sum(dh1 * xh, axis=0, keepdims=True))
    add_row(8, jnp.sum(dh1, axis=0, keepdims=True))
    add_row(16, jnp.sum(dh2 * xh, axis=0, keepdims=True))
    add_row(24, jnp.sum(dh2, axis=0, keepdims=True))
    add_row(40, jnp.sum(dc.astype(F32), axis=0, keepdims=True))
    add_row(43, jnp.sum(du.astype(F32), axis=0, keepdims=True))


def backward(e, kept, wa, wb, at, masks):
    xh, qkv, prob, _, _, slope, vectors = kept
    return pl.pallas_call(
        backward_kernel,
        grid=(ROWS // STEP,),
        in_specs=[row_spec(D), row_spec(D), row_spec(QKV_R), PROB_SPEC, row_spec(FF_R)]
        + [WA_SPEC]
        + wb_specs(at)
        + [VEC_SPEC]
        + [row_spec(128)] * 3,
        out_specs=[NEAR_SPEC, FAR_SPEC, row_spec(QKV_R), row_spec(FF_R), whole_spec((64, 128))],
        out_shape=[
            HALF,
            HALF,
            rows_of(QKV_R, BF),
            rows_of(FF_R, BF),
            jax.ShapeDtypeStruct((64, 128), F32),
        ],
        scratch_shapes=HELD,
        compiler_params=params(LARGE),
        name="backward",
    )(e, xh, qkv, prob, slope, wa, wb, wb, wb, vectors, *masks[1:])


def grad_in_kernel(xh_ref, vec_ref, dc_ref, du_ref, side_ref, out_ref):
    xh = xh_ref[...].astype(F32)
    h1 = (xh * vec_ref[0:1] + vec_ref[1:2]).astype(BF)
    h2 = (xh * vec_ref[2:3] + vec_ref[3:4]).astype(BF)
    out_ref[:, :, :QKV_R] = dot_tn(h1, dc_ref[...]).astype(BF).reshape(4, 64, QKV_R)
    out_ref[:, :, QKV_R:A_LANES] = dot_tn(h2, du_ref[...]).astype(BF).reshape(4, 64, FF_R)
    out_ref[:, :, A_LANES:] = jnp.broadcast_to(side_ref[...].astype(BF)[None], (4, 64, 128))


def grad_all_kernel(xh_ref, vec_ref, dc_ref, du_ref, side_ref, shares_ref, out_ref):
    grad_in_kernel(xh_ref, vec_ref, dc_ref, du_ref, side_ref, out_ref.at[:, :64])
    out_ref[:, 64:] = shares_ref[...]


def grad_all(xh, vectors, dc, du, side, shares):
    return pl.pallas_call(
        grad_all_kernel,
        grid=(4,),
        in_specs=[
            pl.BlockSpec((ROWS, 256), lambda i: (0, i)),
            pl.BlockSpec((16, 256), lambda i: (0, i)),
            whole_spec((ROWS, QKV_R)),
            whole_spec((ROWS, FF_R)),
            whole_spec((64, 128)),
            pl.BlockSpec((4, 48, D), lambda i: (i, 0, 0)),
        ],
        out_specs=pl.BlockSpec((4, 112, D), lambda i: (i, 0, 0)),
        out_shape=jax.ShapeDtypeStruct((SHARDS, 112, D), BF),
        compiler_params=params(),
        name="grad_all",
    )(xh, vectors, dc, du, side, shares)


def grad_in(xh, vectors, dc, du, side):
    return pl.pallas_call(
        grad_in_kernel,
        grid=(4,),
        in_specs=[
            pl.BlockSpec((ROWS, 256), lambda i: (0, i)),
            pl.BlockSpec((16, 256), lambda i: (0, i)),
            whole_spec((ROWS, QKV_R)),
            whole_spec((ROWS, FF_R)),
            whole_spec((64, 128)),
        ],
        out_specs=pl.BlockSpec((4, 64, D), lambda i: (i, 0, 0)),
        out_shape=jax.ShapeDtypeStruct((SHARDS, 64, D), BF),
        compiler_params=params(),
        name="grad_in",
    )(xh, vectors, dc, du, side)


def grad_out_kernel(o_ref, act_ref, *refs):
    pieces, (out_ref, e_ref) = refs[:REPS], refs[REPS:]
    e = jnp.concatenate([piece[...] for piece in pieces], axis=0)
    e_ref[...] = e
    down = dot_tn(act_ref[...], e).reshape(SHARDS, UNIT, 256)
    dense = dot_tn(o_ref[...], e).reshape(SHARDS, 8, 256)
    empty = jnp.zeros((SHARDS, 8, 256), F32)
    out_ref[...] = jnp.concatenate([down, dense, empty], axis=1).astype(BF)


def grad_out_of(attended, act, blocks, at):
    return pl.pallas_call(
        grad_out_kernel,
        grid=(4,),
        in_specs=[
            whole_spec((ROWS, 128)),
            whole_spec((ROWS, FF_R)),
        ]
        + [pl.BlockSpec((TOK, 256), lambda i: (at, i))] * REPS,
        out_specs=[
            pl.BlockSpec((SHARDS, 48, 256), lambda i: (0, 0, i)),
            pl.BlockSpec((ROWS, 256), lambda i: (0, i)),
        ],
        out_shape=[jax.ShapeDtypeStruct((SHARDS, 48, D), BF), rows_of(D, BF)],
        compiler_params=params(),
        name="grad_out",
    )(attended, act, *blocks)


def standardize(x):
    centered = x - jnp.mean(x, axis=-1, keepdims=True)
    scale = lax.rsqrt(jnp.mean(centered * centered, axis=-1, keepdims=True) + EPS)
    return centered * scale, scale


def in_order(near, far, c):
    return jnp.stack([jnp.where(c == 0, near, far), jnp.where(c == 0, far, near)], axis=1).reshape((REPS,) + near.shape[1:])


def per_device(
    tokens, doc_ids, grad_out, norm_gains, shifts, qkv_weight, qkv_bias, dense_weight, up_weight, up_bias, down_weight
):
    r = lax.axis_index("rep").astype(jnp.int32)
    s = lax.axis_index("shard").astype(jnp.int32)
    y, c = r // 2, r % 2
    place = jnp.stack([r, s])

    dense = lax.dynamic_slice_in_dim(dense_weight, 8 * r, 8, 1)
    dense = lax.ppermute(dense, ("rep", "shard"), DENSE_IN)
    first, late, packed_b = pack(place, qkv_weight, up_weight, down_weight, norm_gains, shifts, qkv_bias, up_bias)
    packed_b = jnp.concatenate([packed_b, dense, jnp.zeros((LAYERS, 8, D), BF)], axis=1)
    wa0 = exchange_shard(first)
    wb0 = lax.all_gather(packed_b[0], "shard", axis=0)

    current = tokens.astype(F32)
    hat, scale = standardize(current)
    live = (doc_ids >= 0).astype(F32)[:, None]
    grad_y = grad_out.astype(F32) * live
    marks = jnp.pad(doc_ids.astype(BF).reshape(1, TOK), ((0, 15), (0, D - TOK)))
    opened = gather_rep(jnp.concatenate([hat.astype(BF), grad_y.astype(BF), marks], axis=0))
    masks = token_tables(opened)

    late = jnp.concatenate([late, packed_b[1]], axis=0)
    late, wa0, opened = lax.optimization_barrier((late, wa0, opened))
    late = lax.all_gather(late, "shard", axis=0)

    saved0 = inner(opened, wa0, masks)
    own, moved = scatter_rep(*outer(saved0[3], saved0[4], wb0, 0))
    hat0, scale0 = hat, scale
    current = current + total_of(own, moved) + saved0[6][4:5] + saved0[6][5:6]
    hat, scale = standardize(current)
    saved1 = inner(gather_rep(hat.astype(BF)), late, masks)

    def input_grad_of(dy, hat, scale, total):
        shared = jnp.mean(total, axis=-1, keepdims=True)
        along = jnp.mean(total * hat, axis=-1, keepdims=True)
        return dy + scale * (total - shared - hat * along)

    shares, e = grad_out_of(saved1[3], saved1[4], opened, 1)
    raw_b1 = exchange_shard(shares)
    near, far, *grads = backward(e, saved1, late, late, 4, masks)
    own, moved = scatter_rep(near, far)
    grad_y = input_grad_of(grad_y, hat, scale, total_of(own, moved))
    blocks = gather_rep(grad_y.astype(BF))
    grads, _ = lax.optimization_barrier((grads, blocks[1]))
    raw_a1 = exchange_shard(grad_in(saved1[0], saved1[6], *grads))
    attended, act, _ = lax.optimization_barrier((saved1[3], saved1[4], blocks[1]))
    part = outer(attended, act, late, 4)

    shares, e = grad_out_of(saved0[3], saved0[4], blocks, 0)
    near, far, *grads = backward(e, saved0, wa0, wb0, 0, masks)
    raw0 = exchange_shard(grad_all(saved0[0], saved0[6], *grads, shares))
    part, near, raw_a1, raw_b1, _ = lax.optimization_barrier((part, near, raw_a1, raw_b1, grads))
    in_own, in_moved = scatter_rep(near, far)
    out_own, out_moved = scatter_rep(*part)
    sum_a1, sum_b1 = add_up(raw_a1), add_up(raw_b1)
    early = jnp.concatenate([sum_a1, sum_b1[:UNIT]], axis=0)
    early = in_y_order([early] + [fetch_y(early, k) for k in (1, 2, 3)], y)
    early = (early, flip_core(early))
    grad_qkv, grad_up, grad_down = unpack_early(place, *early)
    raw0, out_moved, in_moved = lax.optimization_barrier((raw0, out_moved, in_moved))
    sum0 = add_up(raw0)
    grad_y = input_grad_of(grad_y, hat0, scale0, total_of(in_own, in_moved))
    output = (current + total_of(out_own, out_moved) + saved1[6][4:5] + saved1[6][5:6]).astype(BF)
    moved = jnp.concatenate([sum_b1[UNIT:], sum0[64 + UNIT :]], axis=0)
    moved = lax.ppermute(moved, ("rep", "shard"), DENSE_OUT)
    ending = jnp.concatenate([sum0[: 64 + UNIT], moved], axis=0)
    ending = along_y(jnp.broadcast_to(ending[None], (4, TOK, D)))
    ending, grad_qkv, grad_up, grad_down = lax.optimization_barrier((ending, grad_qkv, grad_up, grad_down))
    ending = (ending, flip_core(ending))
    grad_qkv, grad_up, grad_down, grad_dense = unpack_late(place, *ending, grad_qkv, grad_up, grad_down)

    pieces = (ending, early)
    sides = [in_order(p[0][:, :47, A_LANES:], p[1][:, :47, A_LANES:], c).astype(F32) for p in pieces]
    side = jnp.stack(sides)
    sums = jnp.sum(side[:, :, :32], axis=1)
    sums = jnp.concatenate([sums, side[:, 0, 32:40]], axis=1).reshape(LAYERS, 5, D)
    sums = lax.dynamic_slice_in_dim(sums, 64 * s, 64, 2)
    grad_gains = jnp.stack([sums[:, 0], sums[:, 2]], axis=1)
    grad_shifts = jnp.stack([sums[:, 1], sums[:, 3], sums[:, 4], sums[:, 4]], axis=1)
    qkv_b = jnp.swapaxes(side[:, :, 40:43], 1, 2).reshape(LAYERS, 3 * D)
    grad_qkv_bias = lax.dynamic_slice_in_dim(qkv_b, 192 * s, 192, 1)
    up_b = side[:, :, 43:].reshape(LAYERS, REPS, FF_R)
    grad_up_bias = lax.dynamic_slice_in_dim(up_b, UNIT * s, UNIT, 2).reshape(LAYERS, 256)
    return (
        output,
        grad_y,
        grad_gains,
        grad_shifts,
        grad_qkv,
        grad_qkv_bias,
        grad_dense,
        grad_up,
        grad_up_bias,
        grad_down,
    )


def solution(mesh):
    return jax.shard_map(
        per_device,
        mesh=mesh,
        in_specs=(
            P(("rep", "shard"), None),
            P(("rep", "shard")),
            P(("rep", "shard"), None),
            P(None, None, "shard"),
            P(None, None, "shard"),
            P(None, "shard", None),
            P(None, "shard"),
            P(None, "shard", None),
            P(None, "shard", None),
            P(None, "shard"),
            P(None, "shard", None),
        ),
        out_specs=(
            P(("rep", "shard"), None),
            P(("rep", "shard"), None),
            P(None, None, "shard"),
            P(None, None, "shard"),
            P(None, "shard", None),
            P(None, "shard"),
            P(None, "shard", None),
            P(None, "shard", None),
            P(None, "shard"),
            P(None, "shard", None),
        ),
        check_vma=False,
    )
```

profile of v0, /device:TPU:0, one launch (start us, length us, event | category | flops | bytes accessed | tf_op | source)
XLA Modules:
  0.0 366.1 jit_solution(14010827364344450976)
XLA Ops:
  15.0 13.7 %all-to-all-start = ((bf16[16,64,1024]{2,1,0:T(8,128)(2,1)}), bf16[16,64,1024]{2,1,0:T(8,128)(2,1)}, u32[]{:S(2)}, u32[]{:S(2)}) async-start(bf16[16,64,1024]{2,1,0:T(8,128)(2,1)} %get-tuple-element.105), calls=%async_computation | async-start | bytes 4194304 | tf_op jit(solution)/shard_map/all_to_all | solution.py:80
  33.9 20.4 %collective-permute-done.1.refs_1_ = bf16[272,1024]{1,0:T(8,128)(2,1)S(1)} collective-permute-done((bf16[272,1024]{1,0:T(8,128)(2,1)S(1)}, bf16[272,1024]{1,0:T(8,128)(2,1)S(1)}, u32[]{:S(2)}, u32[]{:S(2)}) %collective-permute-start.1) | collective-permute-done | bytes 557088 | tf_op jit(solution)/shard_map/ppermute | solution.py:42
  65.1 10.1 %inner.2 = (bf16[1024,1024]{1,0:T(8,128)(2,1)}, bf16[1024,384]{1,0:T(8,128)(2,1)}, f32[8,2,128,128]{3,2,1,0:T(8,128)}, bf16[1024,128]{1,0:T(8,128)(2,1)}, bf16[1...) custom-call(bf16[272,1024]{1,0:T(8,128)(2,1)} %copy-done.5, bf16[272,1024]{1,0:T(8,128)(2,1)} %copy-done.12, ...), custom_call_target="tpu_custom_call" | custom-call | tf_op jit(solution)/shard_map/inner/pallas_call | solution.py:430
  75.2 7.3 %all-gather.4.cloned.1.call-done.down0_ref.down1_ref.dense_ref = bf16[16,48,1024]{2,1,0:T(8,128)(2,1)} async-done(((bf16[1,48,1024]{2,1,0:T(8,128)(2,1)}), bf16[16,48,1024]{2,1,0:T(8,128)(2,1)}) %all-gather.4.cloned.1.call-update) | async-done | bytes 1572880 | tf_op jit(solution)/shard_map/all_gather | solution.py:654
  97.8 4.7 %collective-permute-done.10 = bf16[128,1024]{1,0:T(8,128)(2,1)S(1)} collective-permute-done((bf16[128,1024]{1,0:T(8,128)(2,1)S(1)}, bf16[128,1024]{1,0:T(8,128)(2,1)S(1)}, u32[]{:S(2)}, u32[]{:S(2)}) %collective-permute-start.10) | collective-permute-done | bytes 262176 | tf_op jit(solution)/shard_map/ppermute | solution.py:42
  102.5 5.0 %collective-permute-done.11 = bf16[128,1024]{1,0:T(8,128)(2,1)S(1)} collective-permute-done((bf16[128,1024]{1,0:T(8,128)(2,1)S(1)}, bf16[128,1024]{1,0:T(8,128)(2,1)S(1)}, u32[]{:S(2)}, u32[]{:S(2)}) %collective-permute-start.11) | collective-permute-done | bytes 262176 | tf_op jit(solution)/shard_map/ppermute | solution.py:42
  112.6 9.7 %collective-permute-done.12.refs_1_ = bf16[128,1024]{1,0:T(8,128)(2,1)S(1)} collective-permute-done((bf16[128,1024]{1,0:T(8,128)(2,1)S(1)}, bf16[128,1024]{1,0:T(8,128)(2,1)S(1)}, u32[]{:S(2)}, u32[]{:S(2)}) %collective-permute-start.12) | collective-permute-done | bytes 262176 | tf_op jit(solution)/shard_map/ppermute | solution.py:42
  127.5 6.4 %all-gather.6.cloned.1.call-done = bf16[1792,1024]{1,0:T(8,128)(2,1)} async-done(((bf16[112,1024]{1,0:T(8,128)(2,1)}), bf16[1792,1024]{1,0:T(8,128)(2,1)}) %all-gather.6.cloned.1.call-update) | async-done | bytes 3670032 | tf_op jit(solution)/shard_map/all_gather | solution.py:666
  134.0 10.2 %inner.3 = (bf16[1024,1024]{1,0:T(8,128)(2,1)}, bf16[1024,384]{1,0:T(8,128)(2,1)}, f32[8,2,128,128]{3,2,1,0:T(8,128)}, bf16[1024,128]{1,0:T(8,128)(2,1)}, bf16[1...) custom-call(bf16[128,1024]{1,0:T(8,128)(2,1)} %copy-done.53, bf16[128,1024]{1,0:T(8,128)(2,1)} %copy-done.60, ...), custom_call_target="tpu_custom_call" | custom-call | tf_op jit(solution)/shard_map/inner/pallas_call | solution.py:430
  146.4 4.6 %grad_out.2 = (bf16[16,48,1024]{2,1,0:T(8,128)(2,1)}, bf16[1024,1024]{1,0:T(8,128)(2,1)S(1)}) custom-call(bf16[1024,128]{1,0:T(8,128)(2,1)S(1)} %copy-done.28, bf16[1024,512]{1,0:T(8,128)(2,1)S(1)} %copy-done.20, bf16[272,1024]{1,0:T(8,128)(2,1)S(1)} %copy-done.6, bf16[272,1024]{1,0:T(8,128)(2,1)S(1)} %copy-done.13, bf16[272,1024]{1,0:T(8,128)(2,1)S(1)} %copy-done.15, ...), custom_call_target="tpu_custom_call" | custom-call | tf_op jit(solution)/shard_map/grad_out/pallas_call | solution.py:613
  152.3 15.3 %backward.2 = (bf16[512,1024]{1,0:T(8,128)(2,1)}, bf16[512,1024]{1,0:T(8,128)(2,1)}, bf16[1024,384]{1,0:T(8,128)(2,1)}, bf16[1024,512]{1,0:T(8,128)(2,1)}, f32[64,128]{1,0:T(8,128)}) custom-call(bf16[1024,1024]{1,0:T(8,128)(2,1)} %copy-done.24, bf16[1024,1024]{1,0:T(8,128)(2,1)} %get-tuple-element.132.xh_ref, bf16[1024,384]{1,0:T(8,128)(2,1)} %get-tuple-element.133.qkv_ref, ...), custom_call_target="tpu_custom_call" | custom-call | tf_op jit(solution)/shard_map/backward/pallas_call | solution.py:529
  167.7 4.9 %all-to-all-start.2 = ((bf16[16,48,1024]{2,1,0:T(8,128)(2,1)}), bf16[16,48,1024]{2,1,0:T(8,128)(2,1)}, u32[]{:S(2)}, u32[]{:S(2)}) async-start(bf16[16,48,1024]{2,1,0:T(8,128)(2,1)} %get-tuple-element.159), calls=%async_computation.2 | async-start | bytes 3145728 | tf_op jit(solution)/shard_map/all_to_all | solution.py:80
  182.5 6.6 %collective-permute-done.21 = bf16[128,1024]{1,0:T(8,128)(2,1)S(1)} collective-permute-done((bf16[128,1024]{1,0:T(8,128)(2,1)S(1)}, bf16[128,1024]{1,0:T(8,128)(2,1)S(1)}, u32[]{:S(2)}, u32[]{:S(2)}) %collective-permute-start.21) | collective-permute-done | bytes 262176 | tf_op jit(solution)/shard_map/ppermute | solution.py:42
  192.8 5.9 %collective-permute-done.23.refs_1_ = bf16[128,1024]{1,0:T(8,128)(2,1)S(1)} collective-permute-done((bf16[128,1024]{1,0:T(8,128)(2,1)S(1)}, bf16[128,1024]{1,0:T(8,128)(2,1)S(1)}, u32[]{:S(2)}, u32[]{:S(2)}) %collective-permute-start.23) | collective-permute-done | bytes 262176 | tf_op jit(solution)/shard_map/ppermute | solution.py:42
  202.9 7.0 %all-to-all-start.1 = ((bf16[16,64,1024]{2,1,0:T(8,128)(2,1)}), bf16[16,64,1024]{2,1,0:T(8,128)(2,1)}, u32[]{:S(2)}, u32[]{:S(2)}) async-start(bf16[16,64,1024]{2,1,0:T(8,128)(2,1)} %grad_in.1), calls=%async_computation.1 | async-start | bytes 4194304 | tf_op jit(solution)/shard_map/all_to_all | solution.py:80
  215.0 5.7 %collective-permute-done.24.refs_2_ = bf16[128,1024]{1,0:T(8,128)(2,1)S(1)} collective-permute-done((bf16[128,1024]{1,0:T(8,128)(2,1)S(1)}, bf16[128,1024]{1,0:T(8,128)(2,1)S(1)}, u32[]{:S(2)}, u32[]{:S(2)}) %collective-permute-start.24) | collective-permute-done | bytes 262176 | tf_op jit(solution)/shard_map/ppermute | solution.py:42
  230.0 15.4 %backward.3 = (bf16[512,1024]{1,0:T(8,128)(2,1)}, bf16[512,1024]{1,0:T(8,128)(2,1)}, bf16[1024,384]{1,0:T(8,128)(2,1)}, bf16[1024,512]{1,0:T(8,128)(2,1)}, f32[64,128]{1,0:T(8,128)}) custom-call(bf16[1024,1024]{1,0:T(8,128)(2,1)} %copy-done.25, bf16[1024,1024]{1,0:T(8,128)(2,1)} %get-tuple-element.148.xh_ref, bf16[1024,384]{1,0:T(8,128)(2,1)} %get-tuple-element.149.qkv_ref, ...), custom_call_target="tpu_custom_call" | custom-call | tf_op jit(solution)/shard_map/backward/pallas_call | solution.py:529
  253.9 7.0 %all-to-all-start.3 = ((bf16[16,112,1024]{2,1,0:T(8,128)(2,1)}), bf16[16,112,1024]{2,1,0:T(8,128)(2,1)}, u32[]{:S(2)}, u32[]{:S(2)}) async-start(bf16[16,112,1024]{2,1,0:T(8,128)(2,1)} %copy-done.4), calls=%async_computation.3 | async-start | bytes 7340032 | tf_op jit(solution)/shard_map/all_to_all | solution.py:80
  292.7 5.1 %collective-permute-done.36 = bf16[128,1024]{1,0:T(8,128)(2,1)S(1)} collective-permute-done((bf16[128,1024]{1,0:T(8,128)(2,1)S(1)}, bf16[128,1024]{1,0:T(8,128)(2,1)S(1)}, u32[]{:S(2)}, u32[]{:S(2)}) %collective-permute-start.36) | collective-permute-done | bytes 262176 | tf_op jit(solution)/shard_map/ppermute | solution.py:42
  298.8 4.3 %collective-permute-done.31 = bf16[128,1024]{1,0:T(8,128)(2,1)S(1)} collective-permute-done((bf16[128,1024]{1,0:T(8,128)(2,1)S(1)}, bf16[128,1024]{1,0:T(8,128)(2,1)S(1)}, u32[]{:S(2)}, u32[]{:S(2)}) %collective-permute-start.31) | collective-permute-done | bytes 262176 | tf_op jit(solution)/shard_map/ppermute | solution.py:42
  303.2 4.5 %collective-permute-done.32 = bf16[128,1024]{1,0:T(8,128)(2,1)S(1)} collective-permute-done((bf16[128,1024]{1,0:T(8,128)(2,1)S(1)}, bf16[128,1024]{1,0:T(8,128)(2,1)S(1)}, u32[]{:S(2)}, u32[]{:S(2)}) %collective-permute-start.32) | collective-permute-done | bytes 262176 | tf_op jit(solution)/shard_map/ppermute | solution.py:42
  308.5 5.4 %all-to-all-done.3 = bf16[16,112,1024]{2,1,0:T(8,128)(2,1)} async-done(((bf16[16,112,1024]{2,1,0:T(8,128)(2,1)}), bf16[16,112,1024]{2,1,0:T(8,128)(2,1)}, u32[]{:S(2)}, u32[]{:S(2)}) %all-to-all-start.3) | async-done | bytes 3670048 | tf_op jit(solution)/shard_map/all_to_all | solution.py:80
  318.6 13.5 %all-to-all-start.4 = ((bf16[4,128,1024]{2,1,0:T(8,128)(2,1)}), bf16[4,128,1024]{2,1,0:T(8,128)(2,1)S(1)}, u32[]{:S(2)}, u32[]{:S(2)}) async-start(bf16[4,128,1024]{2,1,0:T(8,128)(2,1)} %broadcast_in_dim.15), calls=%async_computation.4 | async-start | bytes 2097152 | tf_op jit(solution)/shard_map/all_to_all | solution.py:53
  335.5 12.4 %all-to-all-done.4.near_ref = bf16[4,128,1024]{2,1,0:T(8,128)(2,1)S(1)} async-done(((bf16[4,128,1024]{2,1,0:T(8,128)(2,1)}), bf16[4,128,1024]{2,1,0:T(8,128)(2,1)S(1)}, u32[]{:S(2)}, u32[]{:S(2)}) %all-to-all-start.4) | async-done | bytes 1048608 | tf_op jit(solution)/shard_map/all_to_all | solution.py:53
  (315 shorter events, 145.9 us)
Async XLA Ops:
  7.2 75.2 %all-gather.4.cloned.1.call-start = ((), (), s32[]{:S(2)}) async-start(), calls=%async_computation.5 | async-start | bytes 1671168 | tf_op jit(solution)/shard_map/all_gather | solution.py:654
  15.0 45.0 %all-to-all-start = ((bf16[16,64,1024]{2,1,0:T(8,128)(2,1)}), bf16[16,64,1024]{2,1,0:T(8,128)(2,1)}, u32[]{:S(2)}, u32[]{:S(2)}) async-start(bf16[16,64,1024]{2,1,0:T(8,128)(2,1)} %get-tuple-element.105), calls=%async_computation | async-start | bytes 4194304 | tf_op jit(solution)/shard_map/all_to_all | solution.py:80
  28.7 105.1 %all-gather.6.cloned.1.call-start = ((), (), s32[]{:S(2)}) async-start(), calls=%async_computation.6 | async-start | bytes 3899392 | tf_op jit(solution)/shard_map/all_gather | solution.py:666
  29.6 24.7 %collective-permute-start.1 = (bf16[272,1024]{1,0:T(8,128)(2,1)S(1)}, bf16[272,1024]{1,0:T(8,128)(2,1)S(1)}, u32[]{:S(2)}, u32[]{:S(2)}) collective-permute-start(bf16[272,1024]{1,0:T(8,128)(2,1)S(1)} %fusion.6.refs_0_), channel_id=1, source_target_pairs={{32,0},{48,16},{64,32},{80,48},{96,64},{112,80},{0,96},{16,112},{3... | collective-permute-start | bytes 1671176 | tf_op jit(solution)/shard_map/ppermute | solution.py:42
  32.2 22.1 %collective-permute-start.2 = (bf16[272,1024]{1,0:T(8,128)(2,1)S(1)}, bf16[272,1024]{1,0:T(8,128)(2,1)S(1)}, u32[]{:S(2)}, u32[]{:S(2)}) collective-permute-start(bf16[272,1024]{1,0:T(8,128)(2,1)S(1)} %fusion.6.refs_0_), channel_id=1, source_target_pairs={{64,0},{80,16},{96,32},{112,48},{0,64},{16,80},{32,96},{48,112},{6... | collective-permute-start | bytes 1671176 | tf_op jit(solution)/shard_map/ppermute | solution.py:42
  33.9 24.1 %collective-permute-start.3 = (bf16[272,1024]{1,0:T(8,128)(2,1)S(1)}, bf16[272,1024]{1,0:T(8,128)(2,1)S(1)}, u32[]{:S(2)}, u32[]{:S(2)}) collective-permute-start(bf16[272,1024]{1,0:T(8,128)(2,1)S(1)} %fusion.6.refs_0_), channel_id=1, source_target_pairs={{96,0},{112,16},{0,32},{16,48},{32,64},{48,80},{64,96},{80,112},{9... | collective-permute-start | bytes 1671176 | tf_op jit(solution)/shard_map/ppermute | solution.py:42
  33.9 24.9 %collective-permute-start.4 = (bf16[272,1024]{1,0:T(8,128)(2,1)S(1)}, bf16[272,1024]{1,0:T(8,128)(2,1)S(1)}, u32[]{:S(2)}, u32[]{:S(2)}) collective-permute-start(bf16[272,1024]{1,0:T(8,128)(2,1)S(1)} %fusion.6.refs_0_), channel_id=1, source_target_pairs={{16,0},{0,16},{48,32},{32,48},{80,64},{64,80},{112,96},{96,112},{1... | collective-permute-start | bytes 1671176 | tf_op jit(solution)/shard_map/ppermute | solution.py:46
  108.2 14.1 %collective-permute-start.12 = (bf16[128,1024]{1,0:T(8,128)(2,1)S(1)}, bf16[128,1024]{1,0:T(8,128)(2,1)S(1)}, u32[]{:S(2)}, u32[]{:S(2)}) collective-permute-start(bf16[128,1024]{1,0:T(8,128)(2,1)S(1)} %fusion.15.refs_0_), channel_id=1, source_target_pairs={{32,0},{48,16},{64,32},{80,48},{96,64},{112,80},{0,96},{16,112},{3... | collective-permute-start | bytes 786440 | tf_op jit(solution)/shard_map/ppermute | solution.py:42
  111.8 14.2 %collective-permute-start.14 = (bf16[128,1024]{1,0:T(8,128)(2,1)S(1)}, bf16[128,1024]{1,0:T(8,128)(2,1)S(1)}, u32[]{:S(2)}, u32[]{:S(2)}) collective-permute-start(bf16[128,1024]{1,0:T(8,128)(2,1)S(1)} %fusion.15.refs_0_), channel_id=1, source_target_pairs={{96,0},{112,16},{0,32},{16,48},{32,64},{48,80},{64,96},{80,112},{9... | collective-permute-start | bytes 786440 | tf_op jit(solution)/shard_map/ppermute | solution.py:42
  167.7 35.2 %all-to-all-start.2 = ((bf16[16,48,1024]{2,1,0:T(8,128)(2,1)}), bf16[16,48,1024]{2,1,0:T(8,128)(2,1)}, u32[]{:S(2)}, u32[]{:S(2)}) async-start(bf16[16,48,1024]{2,1,0:T(8,128)(2,1)} %get-tuple-element.159), calls=%async_computation.2 | async-start | bytes 3145728 | tf_op jit(solution)/shard_map/all_to_all | solution.py:80
  174.5 14.6 %collective-permute-start.21 = (bf16[128,1024]{1,0:T(8,128)(2,1)S(1)}, bf16[128,1024]{1,0:T(8,128)(2,1)S(1)}, u32[]{:S(2)}, u32[]{:S(2)}) collective-permute-start(bf16[128,1024]{1,0:T(8,128)(2,1)S(1)} %get-tuple-element.141), channel_id=1, source_target_pairs={{64,0},{80,16},{96,32},{112,48},{0,64},{16,80},{32,96},{48,112},{6... | collective-permute-start | bytes 786440 | tf_op jit(solution)/shard_map/ppermute | solution.py:42
  202.9 51.0 %all-to-all-start.1 = ((bf16[16,64,1024]{2,1,0:T(8,128)(2,1)}), bf16[16,64,1024]{2,1,0:T(8,128)(2,1)}, u32[]{:S(2)}, u32[]{:S(2)}) async-start(bf16[16,64,1024]{2,1,0:T(8,128)(2,1)} %grad_in.1), calls=%async_computation.1 | async-start | bytes 4194304 | tf_op jit(solution)/shard_map/all_to_all | solution.py:80
  253.9 60.0 %all-to-all-start.3 = ((bf16[16,112,1024]{2,1,0:T(8,128)(2,1)}), bf16[16,112,1024]{2,1,0:T(8,128)(2,1)}, u32[]{:S(2)}, u32[]{:S(2)}) async-start(bf16[16,112,1024]{2,1,0:T(8,128)(2,1)} %copy-done.4), calls=%async_computation.3 | async-start | bytes 7340032 | tf_op jit(solution)/shard_map/all_to_all | solution.py:80
  260.8 14.1 %collective-permute-start.34 = (bf16[512,1024]{1,0:T(8,128)(2,1)}, bf16[512,1024]{1,0:T(8,128)(2,1)}, u32[]{:S(2)}, u32[]{:S(2)}) collective-permute-start(bf16[512,1024]{1,0:T(8,128)(2,1)} %get-tuple-element.171), channel_id=1, source_target_pairs={{16,0},{0,16},{48,32},{32,48},{80,64},{64,80},{112,96},{96,112},{1... | collective-permute-start | bytes 3145736 | tf_op jit(solution)/shard_map/ppermute | solution.py:46
  266.6 20.4 %collective-permute-start.30 = (bf16[512,1024]{1,0:T(8,128)(2,1)}, bf16[512,1024]{1,0:T(8,128)(2,1)S(1)}, u32[]{:S(2)}, u32[]{:S(2)}) collective-permute-start(bf16[512,1024]{1,0:T(8,128)(2,1)} %get-tuple-element.164), channel_id=1, source_target_pairs={{16,0},{0,16},{48,32},{32,48},{80,64},{64,80},{112,96},{96,112},{1... | collective-permute-start | bytes 3145736 | tf_op jit(solution)/shard_map/ppermute | solution.py:46
  274.1 13.9 %collective-permute-start.41 = (bf16[96,1024]{1,0:T(8,128)(2,1)}, bf16[96,1024]{1,0:T(8,128)(2,1)S(1)}, u32[]{:S(2)}, u32[]{:S(2)}) collective-permute-start(bf16[96,1024]{1,0:T(8,128)(2,1)} %pad_maximum_fusion.2), channel_id=1, source_target_pairs={{96,0},{112,16},{0,32},{16,48},{32,64},{48,80},{64,96},{80,112},{9... | collective-permute-start | bytes 589832 | tf_op jit(solution)/shard_map/ppermute | solution.py:42
  277.7 14.5 %collective-permute-start.35 = (bf16[128,1024]{1,0:T(8,128)(2,1)S(1)}, bf16[128,1024]{1,0:T(8,128)(2,1)S(1)}, u32[]{:S(2)}, u32[]{:S(2)}) collective-permute-start(bf16[128,1024]{1,0:T(8,128)(2,1)S(1)} %get-tuple-element.172), channel_id=1, source_target_pairs={{96,0},{112,16},{0,32},{16,48},{32,64},{48,80},{64,96},{80,112},{9... | collective-permute-start | bytes 786440 | tf_op jit(solution)/shard_map/ppermute | solution.py:42
  280.2 17.6 %collective-permute-start.36 = (bf16[128,1024]{1,0:T(8,128)(2,1)S(1)}, bf16[128,1024]{1,0:T(8,128)(2,1)S(1)}, u32[]{:S(2)}, u32[]{:S(2)}) collective-permute-start(bf16[128,1024]{1,0:T(8,128)(2,1)S(1)} %get-tuple-element.173), channel_id=1, source_target_pairs={{64,0},{80,16},{96,32},{112,48},{0,64},{16,80},{32,96},{48,112},{6... | collective-permute-start | bytes 786440 | tf_op jit(solution)/shard_map/ppermute | solution.py:42
  282.8 16.1 %collective-permute-start.37 = (bf16[128,1024]{1,0:T(8,128)(2,1)S(1)}, bf16[128,1024]{1,0:T(8,128)(2,1)S(1)}, u32[]{:S(2)}, u32[]{:S(2)}) collective-permute-start(bf16[128,1024]{1,0:T(8,128)(2,1)S(1)} %get-tuple-element.174), channel_id=1, source_target_pairs={{32,0},{48,16},{64,32},{80,48},{96,64},{112,80},{0,96},{16,112},{3... | collective-permute-start | bytes 786440 | tf_op jit(solution)/shard_map/ppermute | solution.py:42
  288.0 15.2 %collective-permute-start.31 = (bf16[128,1024]{1,0:T(8,128)(2,1)S(1)}, bf16[128,1024]{1,0:T(8,128)(2,1)S(1)}, u32[]{:S(2)}, u32[]{:S(2)}) collective-permute-start(bf16[128,1024]{1,0:T(8,128)(2,1)S(1)} %get-tuple-element.167), channel_id=1, source_target_pairs={{96,0},{112,16},{0,32},{16,48},{32,64},{48,80},{64,96},{80,112},{9... | collective-permute-start | bytes 786440 | tf_op jit(solution)/shard_map/ppermute | solution.py:42
  288.0 19.7 %collective-permute-start.32 = (bf16[128,1024]{1,0:T(8,128)(2,1)S(1)}, bf16[128,1024]{1,0:T(8,128)(2,1)S(1)}, u32[]{:S(2)}, u32[]{:S(2)}) collective-permute-start(bf16[128,1024]{1,0:T(8,128)(2,1)S(1)} %get-tuple-element.168), channel_id=1, source_target_pairs={{64,0},{80,16},{96,32},{112,48},{0,64},{16,80},{32,96},{48,112},{6... | collective-permute-start | bytes 786440 | tf_op jit(solution)/shard_map/ppermute | solution.py:42
  292.1 16.3 %collective-permute-start.33 = (bf16[128,1024]{1,0:T(8,128)(2,1)S(1)}, bf16[128,1024]{1,0:T(8,128)(2,1)}, u32[]{:S(2)}, u32[]{:S(2)}) collective-permute-start(bf16[128,1024]{1,0:T(8,128)(2,1)S(1)} %get-tuple-element.169), channel_id=1, source_target_pairs={{32,0},{48,16},{64,32},{80,48},{96,64},{112,80},{0,96},{16,112},{3... | collective-permute-start | bytes 786440 | tf_op jit(solution)/shard_map/ppermute | solution.py:42
  297.7 34.4 %collective-permute-start.42 = (bf16[4,96,1024]{2,1,0:T(8,128)(2,1)S(1)}, bf16[4,96,1024]{2,1,0:T(8,128)(2,1)S(1)}, u32[]{:S(2)}, u32[]{:S(2)}) collective-permute-start(bf16[4,96,1024]{2,1,0:T(8,128)(2,1)S(1)} %bitcast_dynamic-update-slice_fusion.near_ref), channel_id=1, source_target_pairs={{16,0},{0,16},{48,32},{32,48},{80,64},{64,80},{112,96},{96,112},{1... | collective-permute-start | bytes 2359304 | tf_op jit(solution)/shard_map/ppermute | solution.py:46
  318.6 29.3 %all-to-all-start.4 = ((bf16[4,128,1024]{2,1,0:T(8,128)(2,1)}), bf16[4,128,1024]{2,1,0:T(8,128)(2,1)S(1)}, u32[]{:S(2)}, u32[]{:S(2)}) async-start(bf16[4,128,1024]{2,1,0:T(8,128)(2,1)} %broadcast_in_dim.15), calls=%async_computation.4 | async-start | bytes 2097152 | tf_op jit(solution)/shard_map/all_to_all | solution.py:53
  (101 other events, 953.2 us)
Sparse Core Ops, SparseCore 0:
  15.1 67.2 all-gather.3
  84.6 49.2 all-gather.5
where the time goes:
time: 370 us; the launch traced here: 366 us
  waiting for transfers between devices  129 us (35%)
  starting transfers between devices  88.4 us (24%)
  Pallas kernels  85.6 us (23%)
  local copies, waits for them, and re-layouts  29.1 us (8%)
  other arithmetic  19.1 us (5%)
  between operations  15.2 us (4%)
    ppermute x24, waiting for transfers between devices, fetch_y(): return lax.ppermute(a, 'rep', take_y(k % 4))  90.3 us
    ppermute x24, starting transfers between devices, fetch_y(): return lax.ppermute(a, 'rep', take_y(k % 4))  38.5 us
    all_to_all x4, starting transfers between devices, exchange_shard(): return lax.all_to_all(a, 'shard', 0, 0, tiled=True)  32.6 us
    pallas_call x2, Pallas kernels, backward(): pl.pallas_call(backward_kernel, grid=(ROWS // STEP,), in_specs=[row_spec(...  30.7 us
    unnamed x147, local copies, waits for them, and re-layouts  23.1 us
    pallas_call x2, Pallas kernels, inner(): pl.pallas_call(inner_kernel, grid=(ROWS // STEP,), in_specs=[whole_spec((...  20.3 us
    all_to_all x1, starting transfers between devices, along_y(): lax.all_to_all(a, 'rep', 0, 0, axis_index_groups=Y_GROUPS, tiled=True)  13.5 us
    all_to_all x1, waiting for transfers between devices, along_y(): lax.all_to_all(a, 'rep', 0, 0, axis_index_groups=Y_GROUPS, tiled=True)  12.4 us
  transfers between devices with their start and end apart: 51, of which 25 were waited for; matrix products, arithmetic and copies ran while one was open for 6% of the time, Pallas kernels for 14%

commit v1 on v0

--- a/solution.py
+++ b/solution.py
@@ -707,7 +707,8 @@
     moved = lax.ppermute(moved, ("rep", "shard"), DENSE_OUT)
     ending = jnp.concatenate([sum0[: 64 + UNIT], moved], axis=0)
     ending = along_y(jnp.broadcast_to(ending[None], (4, TOK, D)))
-    ending, grad_qkv, grad_up, grad_down = lax.optimization_barrier((ending, grad_qkv, grad_up, grad_down))
+    held = lax.optimization_barrier((ending, grad_qkv, grad_up, grad_down, grad_y, output))
+    ending, grad_qkv, grad_up, grad_down, grad_y, output = held
     ending = (ending, flip_core(ending))
     grad_qkv, grad_up, grad_down, grad_dense = unpack_late(place, *ending, grad_qkv, grad_up, grad_down)
 

time: 370 us -> 366 us (0.989)
  starting transfers between devices: 88.4 us -> 82.3 us
  waiting for transfers between devices: 129 us -> 134 us
    ppermute x24, waiting for transfers between devices: 90.3 us -> 100 us  [fetch_y(): return lax.ppermute(a, 'rep', take_y(k % 4))]
    all_to_all x4, waiting for transfers between devices: 5.41 us -> 0.01 us  [exchange_shard(): return lax.all_to_all(a, 'shard', 0, 0, tiled=True)]
    ppermute x24, starting transfers between devices: 38.5 us -> 33.3 us  [fetch_y(): return lax.ppermute(a, 'rep', take_y(k % 4))]
    unnamed x147 -> x145, local copies, waits for them, and re-layouts: 23.1 us -> 22 us
  transfers between devices with their start and end apart: 51 -> 51, of which waited for: 25 -> 24; matrix products, arithmetic and copies ran while one was open for 6% -> 5% of each run, Pallas kernels for 14% -> 14%
where the time goes in v1:
time: 366 us; the launch traced here: 363 us
  waiting for transfers between devices  134 us (37%)
  Pallas kernels  84.4 us (23%)
  starting transfers between devices  82.3 us (22%)
  local copies, waits for them, and re-layouts  27.4 us (7%)
  other arithmetic  19.8 us (5%)
  between operations  15.1 us (4%)
    ppermute x24, waiting for transfers between devices, fetch_y(): return lax.ppermute(a, 'rep', take_y(k % 4))  100 us
    ppermute x24, starting transfers between devices, fetch_y(): return lax.ppermute(a, 'rep', take_y(k % 4))  33.3 us
    all_to_all x4, starting transfers between devices, exchange_shard(): return lax.all_to_all(a, 'shard', 0, 0, tiled=True)  32.6 us
    pallas_call x2, Pallas kernels, backward(): pl.pallas_call(backward_kernel, grid=(ROWS // STEP,), in_specs=[row_spec(...  30.7 us
    unnamed x145, local copies, waits for them, and re-layouts  22 us
    pallas_call x2, Pallas kernels, inner(): pl.pallas_call(inner_kernel, grid=(ROWS // STEP,), in_specs=[whole_spec((...  20.3 us
    all_to_all x1, starting transfers between devices, along_y(): lax.all_to_all(a, 'rep', 0, 0, axis_index_groups=Y_GROUPS, tiled=True)  12.9 us
    all_to_all x1, waiting for transfers between devices, along_y(): lax.all_to_all(a, 'rep', 0, 0, axis_index_groups=Y_GROUPS, tiled=True)  11.8 us
  transfers between devices with their start and end apart: 51, of which 24 were waited for; matrix products, arithmetic and copies ran while one was open for 5% of the time, Pallas kernels for 14%

profile of v1, /device:TPU:0, one launch (start us, length us, event | category | flops | bytes accessed | tf_op | source)
XLA Modules:
  0.0 363.4 jit_solution(17863117805784449453)
XLA Ops:
  15.0 13.7 %all-to-all-start = ((bf16[16,64,1024]{2,1,0:T(8,128)(2,1)}), bf16[16,64,1024]{2,1,0:T(8,128)(2,1)}, u32[]{:S(2)}, u32[]{:S(2)}) async-start(bf16[16,64,1024]{2,1,0:T(8,128)(2,1)} %get-tuple-element.107), calls=%async_computation | async-start | bytes 4194304 | tf_op jit(solution)/shard_map/all_to_all | solution.py:80
  33.9 20.4 %collective-permute-done.1.refs_1_ = bf16[272,1024]{1,0:T(8,128)(2,1)S(1)} collective-permute-done((bf16[272,1024]{1,0:T(8,128)(2,1)S(1)}, bf16[272,1024]{1,0:T(8,128)(2,1)S(1)}, u32[]{:S(2)}, u32[]{:S(2)}) %collective-permute-start.1) | collective-permute-done | bytes 557088 | tf_op jit(solution)/shard_map/ppermute | solution.py:42
  65.0 10.1 %inner.2 = (bf16[1024,1024]{1,0:T(8,128)(2,1)}, bf16[1024,384]{1,0:T(8,128)(2,1)}, f32[8,2,128,128]{3,2,1,0:T(8,128)}, bf16[1024,128]{1,0:T(8,128)(2,1)}, bf16[1...) custom-call(bf16[272,1024]{1,0:T(8,128)(2,1)} %copy-done.5, bf16[272,1024]{1,0:T(8,128)(2,1)} %copy-done.12, ...), custom_call_target="tpu_custom_call" | custom-call | tf_op jit(solution)/shard_map/inner/pallas_call | solution.py:430
  75.1 7.3 %all-gather.4.cloned.1.call-done.down0_ref.down1_ref.dense_ref = bf16[16,48,1024]{2,1,0:T(8,128)(2,1)} async-done(((bf16[1,48,1024]{2,1,0:T(8,128)(2,1)}), bf16[16,48,1024]{2,1,0:T(8,128)(2,1)}) %all-gather.4.cloned.1.call-update) | async-done | bytes 1572880 | tf_op jit(solution)/shard_map/all_gather | solution.py:654
  97.6 4.8 %collective-permute-done.10 = bf16[128,1024]{1,0:T(8,128)(2,1)S(1)} collective-permute-done((bf16[128,1024]{1,0:T(8,128)(2,1)S(1)}, bf16[128,1024]{1,0:T(8,128)(2,1)S(1)}, u32[]{:S(2)}, u32[]{:S(2)}) %collective-permute-start.10) | collective-permute-done | bytes 262176 | tf_op jit(solution)/shard_map/ppermute | solution.py:42
  102.5 5.1 %collective-permute-done.11 = bf16[128,1024]{1,0:T(8,128)(2,1)S(1)} collective-permute-done((bf16[128,1024]{1,0:T(8,128)(2,1)S(1)}, bf16[128,1024]{1,0:T(8,128)(2,1)S(1)}, u32[]{:S(2)}, u32[]{:S(2)}) %collective-permute-start.11) | collective-permute-done | bytes 262176 | tf_op jit(solution)/shard_map/ppermute | solution.py:42
  112.4 9.9 %collective-permute-done.12.refs_1_ = bf16[128,1024]{1,0:T(8,128)(2,1)S(1)} collective-permute-done((bf16[128,1024]{1,0:T(8,128)(2,1)S(1)}, bf16[128,1024]{1,0:T(8,128)(2,1)S(1)}, u32[]{:S(2)}, u32[]{:S(2)}) %collective-permute-start.12) | collective-permute-done | bytes 262176 | tf_op jit(solution)/shard_map/ppermute | solution.py:42
  127.5 6.1 %all-gather.6.cloned.1.call-done = bf16[1792,1024]{1,0:T(8,128)(2,1)} async-done(((bf16[112,1024]{1,0:T(8,128)(2,1)}), bf16[1792,1024]{1,0:T(8,128)(2,1)}) %all-gather.6.cloned.1.call-update) | async-done | bytes 3670032 | tf_op jit(solution)/shard_map/all_gather | solution.py:666
  133.7 10.2 %inner.3 = (bf16[1024,1024]{1,0:T(8,128)(2,1)}, bf16[1024,384]{1,0:T(8,128)(2,1)}, f32[8,2,128,128]{3,2,1,0:T(8,128)}, bf16[1024,128]{1,0:T(8,128)(2,1)}, bf16[1...) custom-call(bf16[128,1024]{1,0:T(8,128)(2,1)} %copy-done.50, bf16[128,1024]{1,0:T(8,128)(2,1)} %copy-done.60, ...), custom_call_target="tpu_custom_call" | custom-call | tf_op jit(solution)/shard_map/inner/pallas_call | solution.py:430
  146.2 4.6 %grad_out.2 = (bf16[16,48,1024]{2,1,0:T(8,128)(2,1)}, bf16[1024,1024]{1,0:T(8,128)(2,1)S(1)}) custom-call(bf16[1024,128]{1,0:T(8,128)(2,1)S(1)} %copy-done.28, bf16[1024,512]{1,0:T(8,128)(2,1)S(1)} %copy-done.20, bf16[272,1024]{1,0:T(8,128)(2,1)S(1)} %copy-done.6, bf16[272,1024]{1,0:T(8,128)(2,1)S(1)} %copy-done.13, bf16[272,1024]{1,0:T(8,128)(2,1)S(1)} %copy-done.15, ...), custom_call_target="tpu_custom_call" | custom-call | tf_op jit(solution)/shard_map/grad_out/pallas_call | solution.py:613
  152.2 15.3 %backward.2 = (bf16[512,1024]{1,0:T(8,128)(2,1)}, bf16[512,1024]{1,0:T(8,128)(2,1)}, bf16[1024,384]{1,0:T(8,128)(2,1)}, bf16[1024,512]{1,0:T(8,128)(2,1)}, f32[64,128]{1,0:T(8,128)}) custom-call(bf16[1024,1024]{1,0:T(8,128)(2,1)} %copy-done.24, bf16[1024,1024]{1,0:T(8,128)(2,1)} %get-tuple-element.135.xh_ref, bf16[1024,384]{1,0:T(8,128)(2,1)} %get-tuple-element.136.qkv_ref, ...), custom_call_target="tpu_custom_call" | custom-call | tf_op jit(solution)/shard_map/backward/pallas_call | solution.py:529
  167.7 4.9 %all-to-all-start.3 = ((bf16[16,48,1024]{2,1,0:T(8,128)(2,1)}), bf16[16,48,1024]{2,1,0:T(8,128)(2,1)}, u32[]{:S(2)}, u32[]{:S(2)}) async-start(bf16[16,48,1024]{2,1,0:T(8,128)(2,1)} %get-tuple-element.165), calls=%async_computation.3 | async-start | bytes 3145728 | tf_op jit(solution)/shard_map/all_to_all | solution.py:80
  182.5 6.6 %collective-permute-done.21 = bf16[128,1024]{1,0:T(8,128)(2,1)S(1)} collective-permute-done((bf16[128,1024]{1,0:T(8,128)(2,1)S(1)}, bf16[128,1024]{1,0:T(8,128)(2,1)S(1)}, u32[]{:S(2)}, u32[]{:S(2)}) %collective-permute-start.21) | collective-permute-done | bytes 262176 | tf_op jit(solution)/shard_map/ppermute | solution.py:42
  192.7 5.9 %collective-permute-done.23.refs_1_ = bf16[128,1024]{1,0:T(8,128)(2,1)S(1)} collective-permute-done((bf16[128,1024]{1,0:T(8,128)(2,1)S(1)}, bf16[128,1024]{1,0:T(8,128)(2,1)S(1)}, u32[]{:S(2)}, u32[]{:S(2)}) %collective-permute-start.23) | collective-permute-done | bytes 262176 | tf_op jit(solution)/shard_map/ppermute | solution.py:42
  198.6 4.2 %grad_in.1 = bf16[16,64,1024]{2,1,0:T(8,128)(2,1)} custom-call(bf16[1024,1024]{1,0:T(8,128)(2,1)S(1)} %copy-done.7, f32[16,1024]{1,0:T(8,128)S(1)} %copy-done.40, bf16[1024,384]{1,0:T(8,128)(2,1)S(1)} %copy-done.36, bf16[1024,512]{1,0:T(8,128)(2,1)S(1)} %copy-done.32, f32[64,128]{1,0:T(8,128)S(1)} %copy-done.43), custom_call_target="tpu_custom_call" | custom-call | tf_op jit(solution)/shard_map/grad_in/pallas_call | solution.py:585
  202.8 7.0 %all-to-all-start.2 = ((bf16[16,64,1024]{2,1,0:T(8,128)(2,1)}), bf16[16,64,1024]{2,1,0:T(8,128)(2,1)}, u32[]{:S(2)}, u32[]{:S(2)}) async-start(bf16[16,64,1024]{2,1,0:T(8,128)(2,1)} %grad_in.1), calls=%async_computation.2 | async-start | bytes 4194304 | tf_op jit(solution)/shard_map/all_to_all | solution.py:80
  214.9 5.7 %collective-permute-done.24.refs_2_ = bf16[128,1024]{1,0:T(8,128)(2,1)S(1)} collective-permute-done((bf16[128,1024]{1,0:T(8,128)(2,1)S(1)}, bf16[128,1024]{1,0:T(8,128)(2,1)S(1)}, u32[]{:S(2)}, u32[]{:S(2)}) %collective-permute-start.24) | collective-permute-done | bytes 262176 | tf_op jit(solution)/shard_map/ppermute | solution.py:42
  229.9 15.4 %backward.3 = (bf16[512,1024]{1,0:T(8,128)(2,1)}, bf16[512,1024]{1,0:T(8,128)(2,1)}, bf16[1024,384]{1,0:T(8,128)(2,1)}, bf16[1024,512]{1,0:T(8,128)(2,1)}, f32[64,128]{1,0:T(8,128)}) custom-call(bf16[1024,1024]{1,0:T(8,128)(2,1)} %copy-done.25, bf16[1024,1024]{1,0:T(8,128)(2,1)} %get-tuple-element.121.xh_ref, bf16[1024,384]{1,0:T(8,128)(2,1)} %get-tuple-element.147.qkv_ref, ...), custom_call_target="tpu_custom_call" | custom-call | tf_op jit(solution)/shard_map/backward/pallas_call | solution.py:529
  253.7 7.0 %all-to-all-start.1 = ((bf16[16,112,1024]{2,1,0:T(8,128)(2,1)}), bf16[16,112,1024]{2,1,0:T(8,128)(2,1)}, u32[]{:S(2)}, u32[]{:S(2)}) async-start(bf16[16,112,1024]{2,1,0:T(8,128)(2,1)} %copy-done.4), calls=%async_computation.1 | async-start | bytes 7340032 | tf_op jit(solution)/shard_map/all_to_all | solution.py:80
  273.9 5.1 %collective-permute-done.39 = bf16[96,1024]{1,0:T(8,128)(2,1)} collective-permute-done((bf16[96,1024]{1,0:T(8,128)(2,1)}, bf16[96,1024]{1,0:T(8,128)(2,1)}, u32[]{:S(2)}, u32[]{:S(2)}) %collective-permute-start.39) | collective-permute-done | bytes 196640 | tf_op jit(solution)/shard_map/ppermute | solution.py:42
  289.7 11.5 %collective-permute-done.35 = bf16[128,1024]{1,0:T(8,128)(2,1)S(1)} collective-permute-done((bf16[128,1024]{1,0:T(8,128)(2,1)S(1)}, bf16[128,1024]{1,0:T(8,128)(2,1)S(1)}, u32[]{:S(2)}, u32[]{:S(2)}) %collective-permute-start.35) | collective-permute-done | bytes 262176 | tf_op jit(solution)/shard_map/ppermute | solution.py:42
  305.0 7.0 %collective-permute-done.31 = bf16[128,1024]{1,0:T(8,128)(2,1)S(1)} collective-permute-done((bf16[128,1024]{1,0:T(8,128)(2,1)S(1)}, bf16[128,1024]{1,0:T(8,128)(2,1)S(1)}, u32[]{:S(2)}, u32[]{:S(2)}) %collective-permute-start.31) | collective-permute-done | bytes 262176 | tf_op jit(solution)/shard_map/ppermute | solution.py:42
  319.2 12.9 %all-to-all-start.4 = ((bf16[4,128,1024]{2,1,0:T(8,128)(2,1)}), bf16[4,128,1024]{2,1,0:T(8,128)(2,1)S(1)}, u32[]{:S(2)}, u32[]{:S(2)}) async-start(bf16[4,128,1024]{2,1,0:T(8,128)(2,1)} %broadcast_in_dim.15), calls=%async_computation.4 | async-start | bytes 2097152 | tf_op jit(solution)/shard_map/all_to_all | solution.py:53
  336.2 11.8 %all-to-all-done.4.near_ref = bf16[4,128,1024]{2,1,0:T(8,128)(2,1)S(1)} async-done(((bf16[4,128,1024]{2,1,0:T(8,128)(2,1)}), bf16[4,128,1024]{2,1,0:T(8,128)(2,1)S(1)}, u32[]{:S(2)}, u32[]{:S(2)}) %all-to-all-start.4) | async-done | bytes 1048608 | tf_op jit(solution)/shard_map/all_to_all | solution.py:53
  (313 shorter events, 135.7 us)
Async XLA Ops:
  7.2 75.2 %all-gather.4.cloned.1.call-start = ((), (), s32[]{:S(2)}) async-start(), calls=%async_computation.5 | async-start | bytes 1671168 | tf_op jit(solution)/shard_map/all_gather | solution.py:654
  15.0 45.0 %all-to-all-start = ((bf16[16,64,1024]{2,1,0:T(8,128)(2,1)}), bf16[16,64,1024]{2,1,0:T(8,128)(2,1)}, u32[]{:S(2)}, u32[]{:S(2)}) async-start(bf16[16,64,1024]{2,1,0:T(8,128)(2,1)} %get-tuple-element.107), calls=%async_computation | async-start | bytes 4194304 | tf_op jit(solution)/shard_map/all_to_all | solution.py:80
  28.7 104.9 %all-gather.6.cloned.1.call-start = ((), (), s32[]{:S(2)}) async-start(), calls=%async_computation.6 | async-start | bytes 3899392 | tf_op jit(solution)/shard_map/all_gather | solution.py:666
  29.6 24.7 %collective-permute-start.1 = (bf16[272,1024]{1,0:T(8,128)(2,1)S(1)}, bf16[272,1024]{1,0:T(8,128)(2,1)S(1)}, u32[]{:S(2)}, u32[]{:S(2)}) collective-permute-start(bf16[272,1024]{1,0:T(8,128)(2,1)S(1)} %fusion.6.refs_0_), channel_id=1, source_target_pairs={{32,0},{48,16},{64,32},{80,48},{96,64},{112,80},{0,96},{16,112},{3... | collective-permute-start | bytes 1671176 | tf_op jit(solution)/shard_map/ppermute | solution.py:42
  32.2 22.1 %collective-permute-start.2 = (bf16[272,1024]{1,0:T(8,128)(2,1)S(1)}, bf16[272,1024]{1,0:T(8,128)(2,1)S(1)}, u32[]{:S(2)}, u32[]{:S(2)}) collective-permute-start(bf16[272,1024]{1,0:T(8,128)(2,1)S(1)} %fusion.6.refs_0_), channel_id=1, source_target_pairs={{64,0},{80,16},{96,32},{112,48},{0,64},{16,80},{32,96},{48,112},{6... | collective-permute-start | bytes 1671176 | tf_op jit(solution)/shard_map/ppermute | solution.py:42
  33.9 24.1 %collective-permute-start.3 = (bf16[272,1024]{1,0:T(8,128)(2,1)S(1)}, bf16[272,1024]{1,0:T(8,128)(2,1)S(1)}, u32[]{:S(2)}, u32[]{:S(2)}) collective-permute-start(bf16[272,1024]{1,0:T(8,128)(2,1)S(1)} %fusion.6.refs_0_), channel_id=1, source_target_pairs={{96,0},{112,16},{0,32},{16,48},{32,64},{48,80},{64,96},{80,112},{9... | collective-permute-start | bytes 1671176 | tf_op jit(solution)/shard_map/ppermute | solution.py:42
  33.9 24.9 %collective-permute-start.4 = (bf16[272,1024]{1,0:T(8,128)(2,1)S(1)}, bf16[272,1024]{1,0:T(8,128)(2,1)S(1)}, u32[]{:S(2)}, u32[]{:S(2)}) collective-permute-start(bf16[272,1024]{1,0:T(8,128)(2,1)S(1)} %fusion.6.refs_0_), channel_id=1, source_target_pairs={{16,0},{0,16},{48,32},{32,48},{80,64},{64,80},{112,96},{96,112},{1... | collective-permute-start | bytes 1671176 | tf_op jit(solution)/shard_map/ppermute | solution.py:46
  94.7 12.8 %collective-permute-start.11 = (bf16[128,1024]{1,0:T(8,128)(2,1)S(1)}, bf16[128,1024]{1,0:T(8,128)(2,1)S(1)}, u32[]{:S(2)}, u32[]{:S(2)}) collective-permute-start(bf16[128,1024]{1,0:T(8,128)(2,1)S(1)} %get-tuple-element.130), channel_id=1, source_target_pairs={{32,0},{48,16},{64,32},{80,48},{96,64},{112,80},{0,96},{16,112},{3... | collective-permute-start | bytes 786440 | tf_op jit(solution)/shard_map/ppermute | solution.py:42
  108.2 14.1 %collective-permute-start.12 = (bf16[128,1024]{1,0:T(8,128)(2,1)S(1)}, bf16[128,1024]{1,0:T(8,128)(2,1)S(1)}, u32[]{:S(2)}, u32[]{:S(2)}) collective-permute-start(bf16[128,1024]{1,0:T(8,128)(2,1)S(1)} %fusion.15.refs_0_), channel_id=1, source_target_pairs={{32,0},{48,16},{64,32},{80,48},{96,64},{112,80},{0,96},{16,112},{3... | collective-permute-start | bytes 786440 | tf_op jit(solution)/shard_map/ppermute | solution.py:42
  111.6 14.4 %collective-permute-start.14 = (bf16[128,1024]{1,0:T(8,128)(2,1)S(1)}, bf16[128,1024]{1,0:T(8,128)(2,1)S(1)}, u32[]{:S(2)}, u32[]{:S(2)}) collective-permute-start(bf16[128,1024]{1,0:T(8,128)(2,1)S(1)} %fusion.15.refs_0_), channel_id=1, source_target_pairs={{96,0},{112,16},{0,32},{16,48},{32,64},{48,80},{64,96},{80,112},{9... | collective-permute-start | bytes 786440 | tf_op jit(solution)/shard_map/ppermute | solution.py:42
  112.4 13.7 %collective-permute-start.15 = (bf16[128,1024]{1,0:T(8,128)(2,1)S(1)}, bf16[128,1024]{1,0:T(8,128)(2,1)S(1)}, u32[]{:S(2)}, u32[]{:S(2)}) collective-permute-start(bf16[128,1024]{1,0:T(8,128)(2,1)S(1)} %fusion.15.refs_0_), channel_id=1, source_target_pairs={{16,0},{0,16},{48,32},{32,48},{80,64},{64,80},{112,96},{96,112},{1... | collective-permute-start | bytes 786440 | tf_op jit(solution)/shard_map/ppermute | solution.py:46
  167.7 35.1 %all-to-all-start.3 = ((bf16[16,48,1024]{2,1,0:T(8,128)(2,1)}), bf16[16,48,1024]{2,1,0:T(8,128)(2,1)}, u32[]{:S(2)}, u32[]{:S(2)}) async-start(bf16[16,48,1024]{2,1,0:T(8,128)(2,1)} %get-tuple-element.165), calls=%async_computation.3 | async-start | bytes 3145728 | tf_op jit(solution)/shard_map/all_to_all | solution.py:80
  174.4 14.6 %collective-permute-start.21 = (bf16[128,1024]{1,0:T(8,128)(2,1)S(1)}, bf16[128,1024]{1,0:T(8,128)(2,1)S(1)}, u32[]{:S(2)}, u32[]{:S(2)}) collective-permute-start(bf16[128,1024]{1,0:T(8,128)(2,1)S(1)} %get-tuple-element.144), channel_id=1, source_target_pairs={{64,0},{80,16},{96,32},{112,48},{0,64},{16,80},{32,96},{48,112},{6... | collective-permute-start | bytes 786440 | tf_op jit(solution)/shard_map/ppermute | solution.py:42
  202.8 50.9 %all-to-all-start.2 = ((bf16[16,64,1024]{2,1,0:T(8,128)(2,1)}), bf16[16,64,1024]{2,1,0:T(8,128)(2,1)}, u32[]{:S(2)}, u32[]{:S(2)}) async-start(bf16[16,64,1024]{2,1,0:T(8,128)(2,1)} %grad_in.1), calls=%async_computation.2 | async-start | bytes 4194304 | tf_op jit(solution)/shard_map/all_to_all | solution.py:80
  253.7 59.6 %all-to-all-start.1 = ((bf16[16,112,1024]{2,1,0:T(8,128)(2,1)}), bf16[16,112,1024]{2,1,0:T(8,128)(2,1)}, u32[]{:S(2)}, u32[]{:S(2)}) async-start(bf16[16,112,1024]{2,1,0:T(8,128)(2,1)} %copy-done.4), calls=%async_computation.1 | async-start | bytes 7340032 | tf_op jit(solution)/shard_map/all_to_all | solution.py:80
  271.5 13.5 %collective-permute-start.34 = (bf16[512,1024]{1,0:T(8,128)(2,1)}, bf16[512,1024]{1,0:T(8,128)(2,1)S(1)}, u32[]{:S(2)}, u32[]{:S(2)}) collective-permute-start(bf16[512,1024]{1,0:T(8,128)(2,1)} %get-tuple-element.172), channel_id=1, source_target_pairs={{16,0},{0,16},{48,32},{32,48},{80,64},{64,80},{112,96},{96,112},{1... | collective-permute-start | bytes 3145736 | tf_op jit(solution)/shard_map/ppermute | solution.py:46
  273.7 15.6 %collective-permute-start.30 = (bf16[512,1024]{1,0:T(8,128)(2,1)}, bf16[512,1024]{1,0:T(8,128)(2,1)S(1)}, u32[]{:S(2)}, u32[]{:S(2)}) collective-permute-start(bf16[512,1024]{1,0:T(8,128)(2,1)} %get-tuple-element.167), channel_id=1, source_target_pairs={{16,0},{0,16},{48,32},{32,48},{80,64},{64,80},{112,96},{96,112},{1... | collective-permute-start | bytes 3145736 | tf_op jit(solution)/shard_map/ppermute | solution.py:46
  284.7 16.5 %collective-permute-start.42 = (bf16[4,96,1024]{2,1,0:T(8,128)(2,1)S(1)}, bf16[4,96,1024]{2,1,0:T(8,128)(2,1)S(1)}, u32[]{:S(2)}, u32[]{:S(2)}) collective-permute-start(bf16[4,96,1024]{2,1,0:T(8,128)(2,1)S(1)} %bitcast_dynamic-update-slice_fusion.near_ref), channel_id=1, source_target_pairs={{16,0},{0,16},{48,32},{32,48},{80,64},{64,80},{112,96},{96,112},{1... | collective-permute-start | bytes 2359304 | tf_op jit(solution)/shard_map/ppermute | solution.py:46
  285.2 16.0 %collective-permute-start.35 = (bf16[128,1024]{1,0:T(8,128)(2,1)S(1)}, bf16[128,1024]{1,0:T(8,128)(2,1)S(1)}, u32[]{:S(2)}, u32[]{:S(2)}) collective-permute-start(bf16[128,1024]{1,0:T(8,128)(2,1)S(1)} %get-tuple-element.173), channel_id=1, source_target_pairs={{96,0},{112,16},{0,32},{16,48},{32,64},{48,80},{64,96},{80,112},{9... | collective-permute-start | bytes 786440 | tf_op jit(solution)/shard_map/ppermute | solution.py:42
  285.3 19.6 %collective-permute-start.36 = (bf16[128,1024]{1,0:T(8,128)(2,1)S(1)}, bf16[128,1024]{1,0:T(8,128)(2,1)S(1)}, u32[]{:S(2)}, u32[]{:S(2)}) collective-permute-start(bf16[128,1024]{1,0:T(8,128)(2,1)S(1)} %get-tuple-element.174), channel_id=1, source_target_pairs={{64,0},{80,16},{96,32},{112,48},{0,64},{16,80},{32,96},{48,112},{6... | collective-permute-start | bytes 786440 | tf_op jit(solution)/shard_map/ppermute | solution.py:42
  287.2 17.7 %collective-permute-start.37 = (bf16[128,1024]{1,0:T(8,128)(2,1)S(1)}, bf16[128,1024]{1,0:T(8,128)(2,1)S(1)}, u32[]{:S(2)}, u32[]{:S(2)}) collective-permute-start(bf16[128,1024]{1,0:T(8,128)(2,1)S(1)} %get-tuple-element.175), channel_id=1, source_target_pairs={{32,0},{48,16},{64,32},{80,48},{96,64},{112,80},{0,96},{16,112},{3... | collective-permute-start | bytes 786440 | tf_op jit(solution)/shard_map/ppermute | solution.py:42
  289.6 22.3 %collective-permute-start.31 = (bf16[128,1024]{1,0:T(8,128)(2,1)S(1)}, bf16[128,1024]{1,0:T(8,128)(2,1)S(1)}, u32[]{:S(2)}, u32[]{:S(2)}) collective-permute-start(bf16[128,1024]{1,0:T(8,128)(2,1)S(1)} %get-tuple-element.168), channel_id=1, source_target_pairs={{96,0},{112,16},{0,32},{16,48},{32,64},{48,80},{64,96},{80,112},{9... | collective-permute-start | bytes 786440 | tf_op jit(solution)/shard_map/ppermute | solution.py:42
  301.3 12.0 %collective-permute-start.33 = (bf16[128,1024]{1,0:T(8,128)(2,1)S(1)}, bf16[128,1024]{1,0:T(8,128)(2,1)}, u32[]{:S(2)}, u32[]{:S(2)}) collective-permute-start(bf16[128,1024]{1,0:T(8,128)(2,1)S(1)} %get-tuple-element.170), channel_id=1, source_target_pairs={{32,0},{48,16},{64,32},{80,48},{96,64},{112,80},{0,96},{16,112},{3... | collective-permute-start | bytes 786440 | tf_op jit(solution)/shard_map/ppermute | solution.py:42
  319.2 28.9 %all-to-all-start.4 = ((bf16[4,128,1024]{2,1,0:T(8,128)(2,1)}), bf16[4,128,1024]{2,1,0:T(8,128)(2,1)S(1)}, u32[]{:S(2)}, u32[]{:S(2)}) async-start(bf16[4,128,1024]{2,1,0:T(8,128)(2,1)} %broadcast_in_dim.15), calls=%async_computation.4 | async-start | bytes 2097152 | tf_op jit(solution)/shard_map/all_to_all | solution.py:53
  (100 other events, 940.9 us)
Sparse Core Ops, SparseCore 0:
  15.1 67.2 all-gather.3
  84.6 49.0 all-gather.5
